TPU v7x, 32 devices: a whole 2x2x4 slice. The times are simulated.
32 devices in a mesh: dp: 8 (over y, x, core), seq: 4 (over z).
Axes of the slice: x: 2, y: 2, z: 4, core: 2. Of those that a mesh axis runs over, the one named last changes fastest.
Arguments:
- block_input: float32 [12288, 768], P(('dp', 'seq')), may hold values from -6 to 6
- embedding: float32 [12288, 768], P(('dp', 'seq')), may hold values from -6 to 6
- earlier_outs: float32 [3, 12288, 768], P(None, ('dp', 'seq')), may hold values from -6 to 6
- dwa_weights: float32 [5], replicated, may hold values from 0.3 to 1.2
- ln1_gain: float32 [768], replicated, may hold values from 0.5 to 1.5
- ln1_bias: float32 [768], replicated, may hold values from -2 to 2
- w_qkv: float32 [768, 2304], P('dp'), may hold values from -0.21875 to 0.21875
- w_out: float32 [768, 768], P('dp'), may hold values from -1.75 to 1.75
- ln2_gain: float32 [768], replicated, may hold values from 0.5 to 1.5
- ln2_bias: float32 [768], replicated, may hold values from -2 to 2
- w_up: float32 [768, 3072], P('dp'), may hold values from -0.21875 to 0.21875
- w_down: float32 [3072, 768], P('dp'), may hold values from -0.109375 to 0.109375
- segments: int32 [8, 1536], P('dp', 'seq'), may hold values from 0 to 11, never falling along the last dimension, each value on 1 to 768 neighbouring positions
- cotangent: float32 [12288, 768], P(('dp', 'seq')), may hold values from -6 to 6
Outputs:
- output: float32 [12288, 768], P(('dp', 'seq'))
- grad_input: float32 [12288, 768], P(('dp', 'seq'))
- grad_dwa: float32 [5], replicated
- grad_ln1_gain: float32 [768], replicated
- grad_ln1_bias: float32 [768], replicated
- grad_qkv: float32 [768, 2304], P('dp')
- grad_wout: float32 [768, 768], P('dp')
- grad_ln2_gain: float32 [768], replicated
- grad_ln2_bias: float32 [768], replicated
- grad_up: float32 [768, 3072], P('dp')
- grad_down: float32 [3072, 768], P('dp')
Inputs may be any that keep to these rules, and one draw needn't show every extreme that they name: `segments`: within a sequence the numbers never fall; equal numbers mark one document, of at most 768 tokens.
All inputs are finite; a program needn't handle non-finite values.
Results may differ from a plain program's by a relative error of at most 0.0003.
Values sent between devices are 32-bit elements; how exact they have to be, the bound alone decides.
No kernel may reach another device: no remote copies, remote signals or barrier semaphores. Data moves between devices by JAX's collectives and lax.ppermute only.
A program may use at most 192 MiB of HBM per device.

v0:
```python
import jax
import jax.numpy as jnp
from jax import lax
from jax.sharding import PartitionSpec as P

HD = 64


precise = lax.Precision.HIGHEST


def matmul(left, right):
    return jnp.dot(left, right, precision=precise)


def inner_rows(left, right):
    return lax.dot_general(left, right, (((0,), (0,)), ((), ())), precision=precise)


def outer_cols(left, right):
    return lax.dot_general(left, right, (((1,), (1,)), ((), ())), precision=precise)


def layer_norm(values, gain, bias):
    row_mean = jnp.mean(values, axis=-1, keepdims=True)
    centred = values - row_mean
    row_var = jnp.mean(centred * centred, axis=-1, keepdims=True)
    return centred * lax.rsqrt(row_var + 1e-05) * gain + bias


def gelu_tanh(values):
    return (
        0.5
        * values
        * (1.0 + jnp.tanh(0.7978845608028654 * (values + 0.044715 * values * values * values)))
    )


def rotary_tables(length, head_dim):
    half_dim = head_dim // 2
    inv_freq = 10000.0 ** (-(jnp.arange(half_dim, dtype=jnp.float32) * 2.0 / head_dim))
    angles = jnp.arange(length, dtype=jnp.float32)[:, None] * inv_freq[None, :]
    angles = jnp.concatenate([angles, angles], axis=1)
    return (jnp.cos(angles), jnp.sin(angles))


def turn_half(values):
    half_dim = values.shape[-1] // 2
    return jnp.concatenate([-values[..., half_dim:], values[..., :half_dim]], axis=-1)


def rotate(values, cosine_tab, sine_tab):
    return values * cosine_tab[:, None, :] + turn_half(values) * sine_tab[:, None, :]


def unrotate(values, cosine_tab, sine_tab):
    return values * cosine_tab[:, None, :] - turn_half(values * sine_tab[:, None, :])


def attention_weights(w_qkv, w_out):
    return (
        lax.all_gather(w_qkv, "dp", axis=0, tiled=True),
        lax.all_gather(w_out, "dp", axis=0, tiled=True),
    )


def mlp_weights(w_up, w_down):
    return (
        lax.all_gather(w_up, "dp", axis=0, tiled=True),
        lax.all_gather(w_down, "dp", axis=0, tiled=True),
    )


def masked_scores(query_block, keys_rot, start, seg_ids, block_rows):
    scale_factor = 1.0 / jnp.sqrt(jnp.float32(query_block.shape[-1]))
    scores = jnp.einsum("qhd,khd->hqk", query_block, keys_rot, precision=precise) * scale_factor
    key_place = jnp.arange(keys_rot.shape[0], dtype=jnp.int32)
    query_place = start + jnp.arange(block_rows, dtype=jnp.int32)
    query_seg = lax.dynamic_slice_in_dim(seg_ids, start, block_rows, 0)
    allowed = (key_place[None, :] <= query_place[:, None]) & (
        seg_ids[None, :] == query_seg[:, None]
    )
    return (jnp.where(allowed[None], scores, -1e30), scale_factor)


def body(
    block_input,
    embedding,
    earlier_outs,
    dwa_weights,
    ln1_gain,
    ln1_bias,
    w_qkv,
    w_out,
    ln2_gain,
    ln2_bias,
    w_up,
    w_down,
    segments,
    cotangent,
):
    groups = lax.axis_size("seq")
    tok_rows = block_input.shape[0]
    model_dim = block_input.shape[1]
    attn_full = attention_weights(w_qkv, w_out)
    normed_one, back_one = jax.vjp(layer_norm, block_input, ln1_gain, ln1_bias)
    packed = matmul(normed_one, attn_full[0]).reshape(tok_rows, 3, model_dim)
    seg_float = segments[0].astype(jnp.float32)
    seg_wide = jnp.broadcast_to(seg_float[:, None, None], (tok_rows, 1, groups))
    heads_qkv, seg_long = (
        lax.all_to_all(packed, "seq", split_axis=2, concat_axis=0, tiled=True),
        lax.all_to_all(seg_wide, "seq", split_axis=2, concat_axis=0, tiled=True),
    )
    seq_len = heads_qkv.shape[0]
    group_width = heads_qkv.shape[2]
    local_heads = group_width // HD
    seg_ids = seg_long[:, 0, 0]
    cosine_tab, sine_tab = rotary_tables(seq_len, HD)
    queries = rotate(heads_qkv[:, 0].reshape(seq_len, local_heads, HD), cosine_tab, sine_tab)
    keys_rot = rotate(heads_qkv[:, 1].reshape(seq_len, local_heads, HD), cosine_tab, sine_tab)
    values_all = heads_qkv[:, 2].reshape(seq_len, local_heads, HD)
    block_rows = min(512, seq_len)
    block_count = seq_len // block_rows

    def attend(index):
        start = index * block_rows
        query_block = lax.dynamic_slice_in_dim(queries, start, block_rows, 0)
        scores, scale_factor = masked_scores(query_block, keys_rot, start, seg_ids, block_rows)
        top_score = jnp.max(scores, axis=-1, keepdims=True)
        expo = jnp.exp(scores - top_score)
        total = jnp.sum(expo, axis=-1, keepdims=True)
        result = jnp.einsum("hqk,khd->qhd", expo / total, values_all, precision=precise)
        return (result, (top_score + jnp.log(total))[..., 0])

    attn_blocks, lse_blocks = lax.map(attend, jnp.arange(block_count, dtype=jnp.int32))
    attn_heads = attn_blocks.reshape(seq_len, local_heads, HD)
    attn_tok = lax.all_to_all(
        attn_heads.reshape(seq_len, group_width), "seq", split_axis=0, concat_axis=1, tiled=True
    )
    resid = block_input + matmul(attn_tok, attn_full[1])
    mlp_full = mlp_weights(w_up, w_down)
    normed_two, back_two = jax.vjp(layer_norm, resid, ln2_gain, ln2_bias)
    up_pre = matmul(normed_two, mlp_full[0])
    act, back_gelu = jax.vjp(gelu_tanh, up_pre)
    block_out = resid + matmul(act, mlp_full[1])
    output = (
        dwa_weights[0] * embedding
        + dwa_weights[1] * earlier_outs[0]
        + dwa_weights[2] * earlier_outs[1]
        + dwa_weights[3] * earlier_outs[2]
        + dwa_weights[4] * block_out
    )
    dwa_local = jnp.stack(
        [
            jnp.sum(cotangent * embedding),
            jnp.sum(cotangent * earlier_outs[0]),
            jnp.sum(cotangent * earlier_outs[1]),
            jnp.sum(cotangent * earlier_outs[2]),
            jnp.sum(cotangent * block_out),
        ]
    )
    grad_block = dwa_weights[4] * cotangent
    mlp_back = mlp_weights(w_up, w_down)
    grad_down_part = inner_rows(act, grad_block)
    grad_act = outer_cols(grad_block, mlp_back[1])
    grad_up_pre = back_gelu(grad_act)[0]
    grad_up_part = inner_rows(normed_two, grad_up_pre)
    grad_normed_two = outer_cols(grad_up_pre, mlp_back[0])
    grad_resid_norm, grad_gain_two, grad_bias_two = back_two(grad_normed_two)
    grad_resid = grad_block + grad_resid_norm
    up_shard, down_shard = (
        lax.psum_scatter(grad_up_part, "dp", scatter_dimension=0, tiled=True),
        lax.psum_scatter(grad_down_part, "dp", scatter_dimension=0, tiled=True),
    )
    attn_back = attention_weights(w_qkv, w_out)
    grad_wout_part = inner_rows(attn_tok, grad_resid)
    grad_attn_tok = outer_cols(grad_resid, attn_back[1])
    grad_heads = lax.all_to_all(grad_attn_tok, "seq", split_axis=1, concat_axis=0, tiled=True)
    grad_heads = grad_heads.reshape(seq_len, local_heads, HD)
    delta_all = jnp.sum(grad_heads * attn_heads, axis=-1)

    def back_block(carry, index):
        grad_keys_acc, grad_values_acc = carry
        start = index * block_rows
        query_block = lax.dynamic_slice_in_dim(queries, start, block_rows, 0)
        grad_block_out = lax.dynamic_slice_in_dim(grad_heads, start, block_rows, 0)
        delta_block = lax.dynamic_slice_in_dim(delta_all, start, block_rows, 0)
        scores, scale_factor = masked_scores(query_block, keys_rot, start, seg_ids, block_rows)
        probs = jnp.exp(scores - lse_blocks[index][..., None])
        grad_values_acc = grad_values_acc + jnp.einsum(
            "hqk,qhd->khd", probs, grad_block_out, precision=precise
        )
        grad_probs = jnp.einsum("qhd,khd->hqk", grad_block_out, values_all, precision=precise)
        grad_scores = probs * (grad_probs - jnp.transpose(delta_block)[:, :, None]) * scale_factor
        grad_query_block = jnp.einsum("hqk,khd->qhd", grad_scores, keys_rot, precision=precise)
        grad_keys_acc = grad_keys_acc + jnp.einsum(
            "hqk,qhd->khd", grad_scores, query_block, precision=precise
        )
        return ((grad_keys_acc, grad_values_acc), grad_query_block)

    zero_heads = jnp.zeros((seq_len, local_heads, HD), jnp.float32)
    (grad_keys_rot, grad_values), grad_query_blocks = lax.scan(
        back_block, (zero_heads, zero_heads), jnp.arange(block_count, dtype=jnp.int32)
    )
    grad_queries = unrotate(
        grad_query_blocks.reshape(seq_len, local_heads, HD), cosine_tab, sine_tab
    )
    grad_keys = unrotate(grad_keys_rot, cosine_tab, sine_tab)
    grad_heads_qkv = jnp.stack(
        [
            grad_queries.reshape(seq_len, group_width),
            grad_keys.reshape(seq_len, group_width),
            grad_values.reshape(seq_len, group_width),
        ],
        axis=1,
    )
    grad_packed = lax.all_to_all(grad_heads_qkv, "seq", split_axis=0, concat_axis=2, tiled=True)
    grad_packed = grad_packed.reshape(tok_rows, 3 * model_dim)
    grad_qkv_part = inner_rows(normed_one, grad_packed)
    grad_normed_one = outer_cols(grad_packed, attn_back[0])
    grad_input_norm, grad_gain_one, grad_bias_one = back_one(grad_normed_one)
    grad_input = grad_resid + grad_input_norm
    qkv_shard, wout_shard = (
        lax.psum_scatter(grad_qkv_part, "dp", scatter_dimension=0, tiled=True),
        lax.psum_scatter(grad_wout_part, "dp", scatter_dimension=0, tiled=True),
    )
    grad_qkv, grad_wout, grad_up, grad_down = lax.psum(
        (qkv_shard, wout_shard, up_shard, down_shard), "seq"
    )
    gain_one, bias_one, gain_two, bias_two, grad_dwa = lax.psum(
        (grad_gain_one, grad_bias_one, grad_gain_two, grad_bias_two, dwa_local), ("dp", "seq")
    )
    return (
        output,
        grad_input,
        grad_dwa,
        gain_one,
        bias_one,
        grad_qkv,
        grad_wout,
        gain_two,
        bias_two,
        grad_up,
        grad_down,
    )


def solution(mesh):
    in_specs = (
        P(("dp", "seq"), None),
        P(("dp", "seq"), None),
        P(None, ("dp", "seq"), None),
        P(),
        P(),
        P(),
        P("dp", None),
        P("dp", None),
        P(),
        P(),
        P("dp", None),
        P("dp", None),
        P("dp", "seq"),
        P(("dp", "seq"), None),
    )
    out_specs = (
        P(("dp", "seq"), None),
        P(("dp", "seq"), None),
        P(),
        P(),
        P(),
        P("dp", None),
        P("dp", None),
        P(),
        P(),
        P("dp", None),
        P("dp", None),
    )
    return jax.shard_map(body, mesh=mesh, in_specs=in_specs, out_specs=out_specs, check_vma=False)
```

profile of v0, /device:TPU:0, one launch (start us, length us, event | category | flops | bytes accessed | tf_op | source)
XLA Modules:
  0.0 1114.9 jit_solution(4232940012747170273)
XLA Ops:
  16.8 44.7 %all-gather.5.cloned.1.call-done = f32[768,2304]{1,0:T(8,128)} async-done(((f32[96,2304]{1,0:T(8,128)}), f32[768,2304]{1,0:T(8,128)}) %all-gather.5.cloned.1.call-update) | async-done | bytes 7077904 | tf_op jit(solution)/shard_map/all_gather | solution.py:62
  61.5 14.2 %fusion.61 = f32[384,2304]{0,1:T(8,128)S(1)} fusion(f32[768,2304]{1,0:T(8,128)} %all-gather.5.cloned.1.call-done, f32[384,768]{1,0:T(8,128)S(1)} %copy-done.1, f32[768]{0:T(1024)S(1)} %copy-done.35, f32[768]{0:T(1024)S(1)} %copy-done.28, f32[384]{0:T(512)S(1)} %fusion.88, f32[384]{0:T(512)S(1)} %broadcast_multiply_fusion.3), kind=kOutput, calls=%fused_computation.104 | convolution fusion | flops 8154906624 | bytes 11805696 | tf_op jit(solution)/shard_map/dot_general | solution.py:13
  85.3 13.5 %all-gather.11.cloned.1.call-start = ((), (), s32[]{:S(2)}) async-start(), calls=%async_computation.12 | async-start | bytes 10616832 | tf_op jit(solution)/shard_map/all_gather | solution.py:70
  101.8 88.6 %all-to-all-done.1 = f32[384,3,768]{0,1,2:T(4,128)} async-done(((f32[384,3,768]{0,1,2:T(4,128)}), f32[384,3,768]{0,1,2:T(4,128)}, u32[]{:S(2)}, u32[]{:S(2)}) %all-to-all-start.1) | async-done | bytes 3538976 | tf_op jit(solution)/shard_map/all_to_all | solution.py:111
  198.4 116.8 %while.27 = (s32[]{:T(128)}, f32[3,512,3,64]{1,0,3,2:T(4,128)}, f32[3,3,512]{2,1,0:T(4,128)}, s32[3]{0:T(128)}, f32[1536,1,1]{0,2,1:T(1,128)S(1)}, /*index=5*/f3...) while((s32[]{:T(128)}, f32[3,512,3,64]{1,0,3,2:T(4,128)}, ...), condition=%wide.region_5.6_spmd, body=%wide.region_2.5_spmd.sunk | while | flops 3652189184 | bytes 41001236 | solution.py:135
  203.1 9.2 fusion.152
  215.2 10.9 fusion.154
  227.2 8.6 dynamic_update_slice.17
  241.9 9.2 fusion.152
  254.0 10.9 fusion.154
  266.0 8.6 dynamic_update_slice.17
  280.7 9.2 fusion.152
  292.7 10.9 fusion.154
  304.8 8.6 dynamic_update_slice.17
  325.4 27.7 %all-to-all-done.2 = f32[4,384,192]{1,2,0:T(8,128)S(1)} async-done(((f32[4,384,192]{1,2,0:T(8,128)}), f32[4,384,192]{1,2,0:T(8,128)S(1)}, u32[]{:S(2)}, u32[]{:S(2)}) %all-to-all-start.2) | async-done | bytes 1179680 | tf_op jit(solution)/shard_map/all_to_all | solution.py:137
  361.1 15.6 %fusion.63 = f32[384,3072]{1,0:T(8,128)} fusion(f32[768,3072]{1,0:T(8,128)} %all-gather.9.cloned.1.call-done, f32[384,768]{1,0:T(8,128)S(1)} %get-tuple-element.273, f32[768]{0:T(1024)S(1)} %copy-done.30, f32[768]{0:T(1024)S(1)} %copy-done.23, f32[384]{0:T(512)} %fusion.89, f32[384]{0:T(512)} %copy-done.31), kind=kOutput, calls=%fused_computation.106 | convolution fusion | flops 10872815616 | bytes 15344640 | tf_op jit(solution)/shard_map/dot_general | solution.py:13
  376.8 18.4 %fusion.40 = f32[384,3072]{1,0:T(8,128)S(1)} fusion(f32[384,3072]{1,0:T(8,128)} %fusion.63, f32[3072,768]{1,0:T(8,128)} %all-gather.11.cloned.1.call-done, f32[384,768]{1,0:T(8,128)S(1)} %copy-done.15, f32[]{:T(128)} %bitcast.11), kind=kOutput, calls=%fused_computation.55 | convolution fusion | flops 10899062784 | bytes 20054020 | tf_op jit(solution)/shard_map/dot_general | solution.py:21
  395.3 12.6 %multiply_reduce_fusion = (f32[768]{0:T(1024)}, f32[384]{0:T(512)S(1)}, f32[768]{0:T(1024)}, f32[384,768]{1,0:T(8,128)S(1)}) fusion(f32[384,768]{1,0:T(8,128)S(1)} %get-tuple-element.273, f32[384]{0:T(512)S(1)} %copy-done.33, f32[384]{0:T(512)S(1)} %copy-done.32, f32[768]{0:T(1024)S(1)} %copy-done.23, f32[384,3072]{1,0:T(8,128)S(1)} %fusion.40, ...), kind=kOutput, calls=%fused_computation.87 | convolution fusion | flops 10873993216 | bytes 16528896 | tf_op jit(solution)/shard_map/dot_general | solution.py:21
  409.5 21.0 %multiply_reduce_fusion.2 = (f32[]{:T(128)}, f32[]{:T(128)}, f32[]{:T(128)}, f32[]{:T(128)}, f32[]{:T(128)}, /*index=5*/f32[384,768]{1,0:T(8,128)}, f32[384,768]{1,0:T(8,128)S(1)}) fusion(f32[384,768]{1,0:T(8,128)S(1)} %copy-done.16, f32[384,768]{1,0:T(8,128)S(1)} %copy-done.45, f32[3,384,768]{2,1,0:T(8,128)} %param.20, f32[]{:T(128)} %bitcast.11, ...), kind=kOutput, calls=%fused_computation.89 | convolution fusion | flops 10887856128 | bytes 24774184 | tf_op jit(solution)/shard_map/dot_general | solution.py:13
  436.1 19.3 %fusion.62 = f32[768,3072]{1,0:T(8,128)} fusion(f32[384,3072]{1,0:T(8,128)} %copy-done.6, f32[384,768]{1,0:T(8,128)S(1)} %get-tuple-element.273, f32[768]{0:T(1024)S(1)} %copy-done.30, f32[768]{0:T(1024)S(1)} %copy-done.23, f32[384]{0:T(512)} %fusion.89, f32[384]{0:T(512)} %copy-done.31), kind=kOutput, calls=%fused_computation.105 | convolution fusion | flops 10872815616 | bytes 15344640 | tf_op jit(solution)/shard_map/dot_general | solution.py:17
  455.4 6.6 fusion.103
  468.6 21.2 %fusion.43 = f32[3072,768]{1,0:T(8,128)} fusion(f32[384,3072]{1,0:T(8,128)} %fusion.63, f32[384,768]{1,0:T(8,128)} %param.31, f32[]{:T(128)} %bitcast.11), kind=kOutput, calls=%fused_computation.60 | convolution fusion | flops 10881368064 | bytes 15335428 | tf_op jit(solution)/shard_map/dot_general | solution.py:17
  501.9 213.6 %while.28 = (s32[]{:T(128)}, f32[1536,3,64]{0,2,1:T(8,128)S(1)}, f32[1536,3,64]{0,2,1:T(8,128)}, f32[3,512,3,64]{1,0,3,2:T(4,128)}, s32[3]{0:T(128)S(1)}, /*inde...) while((s32[]{:T(128)}, f32[1536,3,64]{0,2,1:T(8,128)S(1)}, ...), condition=%wide.region_12.13_spmd.clone, body=%wide.region_11.12_spmd.clone.sunk | while | flops 9084469248 | bytes 108599744 | solution.py:202
  503.6 10.9 fusion.164
  519.4 15.4 %multiply_multiply_fusion.6 = f32[3,512,1536]{2,1,0:T(8,128)} fusion(f32[3,512,1536]{2,1,0:T(8,128)} %fusion.164, f32[1536,3,64]{0,2,1:T(8,128)} %get-tuple-element.507, f32[3,512]{1,0:T(4,128)S(1)} %dynamic-slice_bitcast_fusion.4, f32[3,512]{1,0:T(4,128)S(1)} %dynamic-slice_bitcast_fusion.5, pred[512,1536]{1,0:T(8,128)(4,1)S(1)} %fusion.165, ...), kind=kOutput, calls=%fused_computation.21.clone.1 | convolution fusion | flops 1826095104 | bytes 21245956 | tf_op jit(solution)/shard_map/while/body/eval_jaxpr/qhd,khd->hqk/dot_general | solution.py:193
  534.9 8.5 fusion.166
  543.4 10.6 fusion.167
  555.1 9.2 convolution_bitcast_fusion.3
  564.7 8.8 dynamic_update_slice.18
  574.8 11.0 fusion.164
  590.7 15.3 %multiply_multiply_fusion.6 = f32[3,512,1536]{2,1,0:T(8,128)} fusion(f32[3,512,1536]{2,1,0:T(8,128)} %fusion.164, f32[1536,3,64]{0,2,1:T(8,128)} %get-tuple-element.507, f32[3,512]{1,0:T(4,128)S(1)} %dynamic-slice_bitcast_fusion.4, f32[3,512]{1,0:T(4,128)S(1)} %dynamic-slice_bitcast_fusion.5, pred[512,1536]{1,0:T(8,128)(4,1)S(1)} %fusion.165, ...), kind=kOutput, calls=%fused_computation.21.clone.1 | convolution fusion | flops 1826095104 | bytes 21245956 | tf_op jit(solution)/shard_map/while/body/eval_jaxpr/qhd,khd->hqk/dot_general | solution.py:193
  606.1 8.5 fusion.166
  614.6 10.6 fusion.167
  626.2 9.2 convolution_bitcast_fusion.3
  635.9 8.6 dynamic_update_slice.18
  645.7 10.9 fusion.164
  661.6 15.4 %multiply_multiply_fusion.6 = f32[3,512,1536]{2,1,0:T(8,128)} fusion(f32[3,512,1536]{2,1,0:T(8,128)} %fusion.164, f32[1536,3,64]{0,2,1:T(8,128)} %get-tuple-element.507, f32[3,512]{1,0:T(4,128)S(1)} %dynamic-slice_bitcast_fusion.4, f32[3,512]{1,0:T(4,128)S(1)} %dynamic-slice_bitcast_fusion.5, pred[512,1536]{1,0:T(8,128)(4,1)S(1)} %fusion.165, ...), kind=kOutput, calls=%fused_computation.21.clone.1 | convolution fusion | flops 1826095104 | bytes 21245956 | tf_op jit(solution)/shard_map/while/body/eval_jaxpr/qhd,khd->hqk/dot_general | solution.py:193
  677.0 8.5 fusion.166
  685.5 10.6 fusion.167
  697.1 9.2 convolution_bitcast_fusion.3
  706.8 8.6 dynamic_update_slice.18
  728.4 144.5 %all_to_all.86 = f32[1536,3,192]{2,1,0:T(4,128)} all-to-all(f32[1536,3,192]{2,1,0:T(4,128)} %copy.69), channel_id=1, replica_groups=mesh['dp'=8,'seq'=4] {'seq'}, dimensions={0} | all-to-all | bytes 7077888 | tf_op jit(solution)/shard_map/all_to_all | solution.py:217
  872.9 6.8 copy.71
  879.8 20.3 %fusion.60 = f32[768,2304]{1,0:T(8,128)} fusion(f32[384,2304]{0,1:T(8,128)} %bitcast.164, f32[384,768]{1,0:T(8,128)S(1)} %copy-done.2, f32[768]{0:T(1024)S(1)} %copy-done.36, f32[768]{0:T(1024)S(1)} %copy-done.29, f32[384]{0:T(512)S(1)} %copy-done.27, f32[384]{0:T(512)S(1)} %copy-done.25), kind=kOutput, calls=%fused_computation.103 | convolution fusion | flops 8154906624 | bytes 11805696 | tf_op jit(solution)/shard_map/dot_general | solution.py:17
  900.3 63.7 %reduce-scatter.5.cloned.1.call-done = f32[96,2304]{1,0:T(8,128)} async-done(((f32[768,2304]{1,0:T(8,128)}), f32[96,2304]{1,0:T(8,128)}) %reduce-scatter.5.cloned.1.call-update) | async-done | bytes 884752 | tf_op jit(solution)/shard_map/reduce_scatter | solution.py:224
  967.3 20.8 %multiply_reduce_fusion.1 = (f32[768]{0:T(1024)S(1)}, f32[384]{0:T(512)S(1)}, f32[768]{0:T(1024)S(1)}, f32[384,768]{1,0:T(8,128)S(1)}) fusion(f32[384,768]{1,0:T(8,128)S(1)} %copy-done.2, f32[384]{0:T(512)S(1)} %copy-done.27, f32[384]{0:T(512)S(1)} %copy-done.25, f32[768]{0:T(1024)S(1)} %copy-done.29, f32[384,2304]{0,1:T(8,128)} %bitcast.165, ...), kind=kOutput, calls=%fused_computation.88 | convolution fusion | flops 8156084224 | bytes 12989952 | tf_op jit(solution)/shard_map/dot_general | solution.py:21
  988.2 45.7 %all-reduce = (f32[5]{0:T(128)}, f32[768]{0:T(1024)}, f32[768]{0:T(1024)}, f32[768]{0:T(1024)}, f32[768]{0:T(1024)}) all-reduce(f32[5]{0:T(128)S(1)} %stack.27, f32[768]{0:T(1024)S(1)} %get-tuple-element.180, f32[768]{0:T(1024)S(1)} %get-tuple-element.183, f32[768]{0:T(1024)S(1)} %copy-done.41, ...), channel_id=1, replica_groups=mesh['dp'=8,'seq'=4] {'dp','seq'}, use_global_device_ids=true, to_apply=%region_20.21 | all-reduce | flops 3077 | bytes 24616 | tf_op jit(solution)/shard_map/psum | solution.py:230
  1036.4 66.0 %all-reduce.4.cloned.1.call-done = (f32[96,2304]{1,0:T(8,128)}, f32[96,768]{1,0:T(8,128)}, f32[96,3072]{1,0:T(8,128)}, f32[384,768]{1,0:T(8,128)}) async-done(((f32[96,2304]{1,0:T(8,128)}, f32[96,768]{1,0:T(8,128)}, f32[96,3072]{1,0:T(8,128)}, f32[384,768]{1,0:T(8,128)}), (f32[96,2304]{1,0:T(8,128)}, f32[96,768]{1,0:T(8,128)}, f32[96,3072]{1,0:T(8,128)}, f32[384,768]{1,0:T(8,128)})) %all-reduce.4.cloned.1.call-update) | async-done | bytes 3538960 | tf_op jit(solution)/shard_map/psum | solution.py:227
  (272 shorter events, 141.5 us)
Async XLA Ops:
  7.2 9.2 copy-start.1
  7.2 54.3 %all-gather.5.cloned.1.call-start = ((), (), s32[]{:S(2)}) async-start(), calls=%async_computation.9 | async-start | bytes 7962624 | tf_op jit(solution)/shard_map/all_gather | solution.py:62
  7.9 317.5 %all-gather.7.cloned.1.call-start = ((), (), s32[]{:S(2)}) async-start(), calls=%async_computation.10 | async-start | bytes 2654208 | tf_op jit(solution)/shard_map/all_gather | solution.py:63
  8.7 352.5 %all-gather.9.cloned.1.call-start = ((), (), s32[]{:S(2)}) async-start(), calls=%async_computation.11 | async-start | bytes 10616832 | tf_op jit(solution)/shard_map/all_gather | solution.py:69
  10.0 70.3 %all-to-all-start = ((f32[384,1,4]{0,1,2:T(1,128)}), f32[384,1,4]{0,1,2:T(1,128)S(1)}, u32[]{:S(2)}, u32[]{:S(2)}) async-start(f32[384,1,4]{0,1,2:T(1,128)} %broadcast_in_dim.50), calls=%async_computation | async-start | bytes 12288 | tf_op jit(solution)/shard_map/all_to_all | solution.py:112
  16.4 45.1 %copy-start.28 = (f32[768]{0:T(1024)S(1)}, f32[768]{0:T(1024)}, u32[]{:S(2)}) copy-start(f32[768]{0:T(1024)} %param.22) | copy-start | bytes 9220
  16.4 45.1 %copy-start.35 = (f32[768]{0:T(1024)S(1)}, f32[768]{0:T(1024)}, u32[]{:S(2)}) copy-start(f32[768]{0:T(1024)} %param.23) | copy-start | bytes 9220
  16.5 59.2 %copy-start.24 = (f32[384]{0:T(512)}, f32[384]{0:T(512)S(1)}, u32[]{:S(2)}) copy-start(f32[384]{0:T(512)S(1)} %broadcast_multiply_fusion.3) | copy-start | bytes 4612
  16.8 58.9 %copy-start.37 = (f32[384]{0:T(512)}, f32[384]{0:T(512)S(1)}, u32[]{:S(2)}) copy-start(f32[384]{0:T(512)S(1)} %multiply_reduce_fusion.8) | copy-start | bytes 4612
  16.8 58.9 %copy-start.26 = (f32[384]{0:T(512)}, f32[384]{0:T(512)S(1)}, u32[]{:S(2)}) copy-start(f32[384]{0:T(512)S(1)} %fusion.88) | copy-start | bytes 4612
  80.4 110.1 %all-to-all-start.1 = ((f32[384,3,768]{0,1,2:T(4,128)}), f32[384,3,768]{0,1,2:T(4,128)}, u32[]{:S(2)}, u32[]{:S(2)}) async-start(f32[384,3,768]{0,1,2:T(4,128)} %copy.59), calls=%async_computation.1 | async-start | bytes 9437184 | tf_op jit(solution)/shard_map/all_to_all | solution.py:111
  85.3 291.4 %all-gather.11.cloned.1.call-start = ((), (), s32[]{:S(2)}) async-start(), calls=%async_computation.12 | async-start | bytes 10616832 | tf_op jit(solution)/shard_map/all_gather | solution.py:70
  215.1 10.9 copy-start.22
  253.9 10.9 copy-start.22
  292.7 10.9 copy-start.22
  321.1 32.1 %all-to-all-start.2 = ((f32[4,384,192]{1,2,0:T(8,128)}), f32[4,384,192]{1,2,0:T(8,128)S(1)}, u32[]{:S(2)}, u32[]{:S(2)}) async-start(f32[4,384,192]{1,2,0:T(8,128)} %copy.63), calls=%async_computation.2 | async-start | bytes 2359296 | tf_op jit(solution)/shard_map/all_to_all | solution.py:137
  324.7 575.5 %reduce-scatter.7.cloned.1.call-start = ((), (), s32[]{:S(2)}) async-start(), calls=%async_computation.14 | async-start | bytes 2654208 | tf_op jit(solution)/shard_map/reduce_scatter | solution.py:225
  361.1 15.6 %copy-start.15 = (f32[384,768]{1,0:T(8,128)S(1)}, f32[384,768]{1,0:T(8,128)}, u32[]{:S(2)}) copy-start(f32[384,768]{1,0:T(8,128)} %param.31) | copy-start | bytes 3538948
  376.7 18.5 %copy-start = (f32[768,3072]{1,0:T(8,128)S(1)}, f32[768,3072]{1,0:T(8,128)}, u32[]{:S(2)}) copy-start(f32[768,3072]{1,0:T(8,128)} %all-gather.9.cloned.1.call-done) | copy-start | bytes 28311556
  376.7 18.5 %copy-start.32 = (f32[384]{0:T(512)S(1)}, f32[384]{0:T(512)}, u32[]{:S(2)}) copy-start(f32[384]{0:T(512)} %copy-done.31) | copy-start | bytes 4612
  376.8 18.5 %copy-start.33 = (f32[384]{0:T(512)S(1)}, f32[384]{0:T(512)}, u32[]{:S(2)}) copy-start(f32[384]{0:T(512)} %fusion.89) | copy-start | bytes 4612
  376.8 31.6 %slice-start.3 = ((s8[9437184]{0:T(1024)(128)(4,1)}), s8[4194304]{0:T(1024)(128)(4,1)S(1)}, s32[]{:S(2)}) async-start(s8[9437184]{0:T(1024)(128)(4,1)} %bitcast.183), calls=%async_computation.21 | async-start | bytes 8388608
  376.8 31.6 %slice-start.4 = ((s8[9437184]{0:T(1024)(128)(4,1)}), s8[4194304]{0:T(1024)(128)(4,1)S(1)}, s32[]{:S(2)}) async-start(s8[9437184]{0:T(1024)(128)(4,1)} %bitcast.183), calls=%async_computation.22 | async-start | bytes 8388608
  395.2 12.7 %copy-start.6 = (f32[384,3072]{1,0:T(8,128)}, f32[384,3072]{1,0:T(8,128)S(1)}, u32[]{:S(2)}) copy-start(f32[384,3072]{1,0:T(8,128)S(1)} %fusion.40) | copy-start | bytes 14155780
  395.2 12.7 %copy-start.40 = (f32[384]{0:T(512)S(1)}, f32[384]{0:T(512)}, u32[]{:S(2)}) copy-start(f32[384]{0:T(512)} %copy-done.39) | copy-start | bytes 4612
  395.3 13.2 %copy-start.5 = (f32[384,3072]{1,0:T(8,128)S(1)}, f32[384,3072]{1,0:T(8,128)}, u32[]{:S(2)}) copy-start(f32[384,3072]{1,0:T(8,128)} %fusion.63) | copy-start | bytes 14155780
  395.3 13.2 %slice-start.5 = ((s8[9437184]{0:T(1024)(128)(4,1)}), s8[1048576]{0:T(1024)(128)(4,1)S(1)}, s32[]{:S(2)}) async-start(s8[9437184]{0:T(1024)(128)(4,1)} %bitcast.183), calls=%async_computation.23 | async-start | bytes 2097152
  409.5 21.0 %copy-start.10 = (f32[4,384,192]{1,2,0:T(8,128)S(1)}, f32[4,384,192]{1,2,0:T(8,128)}, u32[]{:S(2)}) copy-start(f32[4,384,192]{1,2,0:T(8,128)} %copy-done.9) | copy-start | bytes 3538948
  430.5 24.9 %copy-start.7 = (f32[384,768]{1,0:T(8,128)}, f32[384,768]{1,0:T(8,128)S(1)}, u32[]{:S(2)}) copy-start(f32[384,768]{1,0:T(8,128)S(1)} %get-tuple-element.252) | copy-start | bytes 3538948
  436.0 464.2 %reduce-scatter.9.cloned.1.call-start = ((), (), s32[]{:S(2)}) async-start(), calls=%async_computation.15 | async-start | bytes 10616832 | tf_op jit(solution)/shard_map/reduce_scatter | solution.py:172
  462.0 31.6 %all-to-all-start.3 = ((f32[384,4,192]{0,2,1:T(8,128)}), f32[384,4,192]{0,2,1:T(8,128)S(1)}, u32[]{:S(2)}, u32[]{:S(2)}) async-start(f32[384,4,192]{0,2,1:T(8,128)} %bitcast.178), calls=%async_computation.3 | async-start | bytes 2359296 | tf_op jit(solution)/shard_map/all_to_all | solution.py:178
  465.5 434.8 %reduce-scatter.11.cloned.1.call-start = ((), (), s32[]{:S(2)}) async-start(), calls=%async_computation.16 | async-start | bytes 10616832 | tf_op jit(solution)/shard_map/reduce_scatter | solution.py:173
  489.8 474.1 %reduce-scatter.5.cloned.1.call-start = ((), (), s32[]{:S(2)}) async-start(), calls=%async_computation.13 | async-start | bytes 7962624 | tf_op jit(solution)/shard_map/reduce_scatter | solution.py:224
  534.8 8.5 copy-start.17
  534.8 20.2 %slice-start = ((s8[9437184]{0:T(1024)(128)(4,1)}), s8[4194304]{0:T(1024)(128)(4,1)S(1)}, s32[]{:S(2)}) async-start(s8[9437184]{0:T(1024)(128)(4,1)} %bitcast.161), calls=%async_computation.18 | async-start | bytes 8388608 | tf_op jit(solution)/shard_map/while
  534.8 20.2 %slice-start.1 = ((s8[9437184]{0:T(1024)(128)(4,1)}), s8[4194304]{0:T(1024)(128)(4,1)S(1)}, s32[]{:S(2)}) async-start(s8[9437184]{0:T(1024)(128)(4,1)} %bitcast.161), calls=%async_computation.19 | async-start | bytes 8388608 | tf_op jit(solution)/shard_map/while
  543.4 11.7 %slice-start.2 = ((s8[9437184]{0:T(1024)(128)(4,1)}), s8[1048576]{0:T(1024)(128)(4,1)S(1)}, s32[]{:S(2)}) async-start(s8[9437184]{0:T(1024)(128)(4,1)} %bitcast.161), calls=%async_computation.20 | async-start | bytes 2097152 | tf_op jit(solution)/shard_map/while
  606.1 8.5 copy-start.17
  606.1 20.2 %slice-start = ((s8[9437184]{0:T(1024)(128)(4,1)}), s8[4194304]{0:T(1024)(128)(4,1)S(1)}, s32[]{:S(2)}) async-start(s8[9437184]{0:T(1024)(128)(4,1)} %bitcast.161), calls=%async_computation.18 | async-start | bytes 8388608 | tf_op jit(solution)/shard_map/while
  606.1 20.2 %slice-start.1 = ((s8[9437184]{0:T(1024)(128)(4,1)}), s8[4194304]{0:T(1024)(128)(4,1)S(1)}, s32[]{:S(2)}) async-start(s8[9437184]{0:T(1024)(128)(4,1)} %bitcast.161), calls=%async_computation.19 | async-start | bytes 8388608 | tf_op jit(solution)/shard_map/while
  614.6 11.6 %slice-start.2 = ((s8[9437184]{0:T(1024)(128)(4,1)}), s8[1048576]{0:T(1024)(128)(4,1)S(1)}, s32[]{:S(2)}) async-start(s8[9437184]{0:T(1024)(128)(4,1)} %bitcast.161), calls=%async_computation.20 | async-start | bytes 2097152 | tf_op jit(solution)/shard_map/while
  677.0 20.1 %slice-start = ((s8[9437184]{0:T(1024)(128)(4,1)}), s8[4194304]{0:T(1024)(128)(4,1)S(1)}, s32[]{:S(2)}) async-start(s8[9437184]{0:T(1024)(128)(4,1)} %bitcast.161), calls=%async_computation.18 | async-start | bytes 8388608 | tf_op jit(solution)/shard_map/while
  677.0 20.1 %slice-start.1 = ((s8[9437184]{0:T(1024)(128)(4,1)}), s8[4194304]{0:T(1024)(128)(4,1)S(1)}, s32[]{:S(2)}) async-start(s8[9437184]{0:T(1024)(128)(4,1)} %bitcast.161), calls=%async_computation.19 | async-start | bytes 8388608 | tf_op jit(solution)/shard_map/while
  685.5 11.6 %slice-start.2 = ((s8[9437184]{0:T(1024)(128)(4,1)}), s8[1048576]{0:T(1024)(128)(4,1)S(1)}, s32[]{:S(2)}) async-start(s8[9437184]{0:T(1024)(128)(4,1)} %bitcast.161), calls=%async_computation.20 | async-start | bytes 2097152 | tf_op jit(solution)/shard_map/while
  900.1 202.3 %all-reduce.4.cloned.1.call-start = ((), (), s32[]{:S(2)}) async-start(), calls=%async_computation.17 | async-start | bytes 7077888 | tf_op jit(solution)/shard_map/psum | solution.py:227
  967.3 20.8 %copy-start.41 = (f32[768]{0:T(1024)S(1)}, f32[768]{0:T(1024)}, u32[]{:S(2)}) copy-start(f32[768]{0:T(1024)} %get-tuple-element.178) | copy-start | bytes 9220
  967.3 20.9 %copy-start.42 = (f32[768]{0:T(1024)S(1)}, f32[768]{0:T(1024)}, u32[]{:S(2)}) copy-start(f32[768]{0:T(1024)} %get-tuple-element.182) | copy-start | bytes 9220
  967.3 66.6 %copy-start.38 = (f32[384]{0:T(512)S(1)}, f32[384]{0:T(512)}, u32[]{:S(2)}) copy-start(f32[384]{0:T(512)} %copy-done.37) | copy-start | bytes 4612
  (31 other events, 88.2 us)
Sparse Core Ops, SparseCore 0:
  9.9 51.5 all-gather.4
  63.4 29.0 all-gather.6
  94.3 58.8 all-gather.8
  154.9 58.8 all-gather.10
  436.1 40.6 reduce-scatter.6
  480.6 76.4 reduce-scatter.8
  561.0 76.4 reduce-scatter.10
  900.3 63.6 reduce-scatter.4
  966.6 135.7 all-reduce.3
where the time goes:
time: 1130 us; the launch traced here: 1110 us
  matrix products  405 us (36%)
  waiting for transfers between devices  297 us (26%)
  blocking collectives  190 us (17%)
  local copies, waits for them, and re-layouts  133 us (12%)
  starting transfers between devices  32.3 us (3%)
  other arithmetic  31.8 us (3%)
  between operations  14.7 us (1%)
    all_to_all x1, blocking collectives, body(): lax.all_to_all(grad_heads_qkv, 'seq', split_axis=0, concat_axis=2, tiled=...  145 us
    all_to_all x1, waiting for transfers between devices, body(): lax.all_to_all(packed, 'seq', split_axis=2, concat_axis=0, tiled=True)  88.6 us
    dot_general x4, matrix products, inner_rows(): lax.dot_general(left, right, (((0,), (0,)), ((), ())), precision=precise)  66.3 us
    psum x1, waiting for transfers between devices, body(): lax.psum((qkv_shard, wout_shard, up_shard, down_shard), 'seq')  66 us
    reduce_scatter x1, waiting for transfers between devices, body(): lax.psum_scatter(grad_qkv_part, 'dp', scatter_dimension=0, tiled=True)  63.7 us
    dot_general x6, matrix products, masked_scores(): jnp.einsum('qhd,khd->hqk', query_block, keys_rot, precision=precise)  60.5 us
    dot_general x4, matrix products, outer_cols(): lax.dot_general(left, right, (((1,), (1,)), ((), ())), precision=precise)  58.4 us
    dynamic_update_slice x12, local copies, waits for them, and re-layouts, body(): lax.map(attend, jnp.arange(block_count, dtype=jnp.int32))  56.6 us
  transfers between devices with their start and end apart: 13, of which 6 were waited for; matrix products, arithmetic and copies ran while one was open for 44% of the time, Pallas kernels for 0%

commit v1 on v0

v1 whole, which is shorter than its diff:
```python
import functools
import math

import jax
import jax.numpy as jnp
import numpy as np
from jax import lax
from jax.experimental import pallas as pl
from jax.experimental.pallas import tpu as pltpu
from jax.sharding import PartitionSpec as P

HD = 64
DOC_MOST = 768
LOG2E = math.log2(math.e)
SCALE = 1.0 / math.sqrt(HD)
NEG = -1e30
F32 = jnp.float32
BF16 = jnp.bfloat16
HIGH = lax.Precision.HIGH
VMEM_LIMIT = 56 * 1024 * 1024
BLK = 128


def params():
    return pltpu.CompilerParams(
        dimension_semantics=("arbitrary",), vmem_limit_bytes=VMEM_LIMIT
    )


def split(values):
    high = values.astype(BF16)
    return high, (values - high.astype(F32)).astype(BF16)


def dot_nn(left, right):
    return lax.dot_general(left, right, (((1,), (0,)), ((), ())), preferred_element_type=F32)


def dot_nt(left, right):
    return lax.dot_general(left, right, (((1,), (1,)), ((), ())), preferred_element_type=F32)


def dot_tn(left, right):
    return lax.dot_general(left, right, (((0,), (0,)), ((), ())), preferred_element_type=F32)


def three(dot, left, right):
    return (
        dot(left[0], right[0]) + dot(left[0], right[1]) + dot(left[1], right[0])
    )


def norm_stats(values):
    row_mean = jnp.mean(values, axis=-1, keepdims=True)
    centred = values - row_mean
    row_var = jnp.mean(centred * centred, axis=-1, keepdims=True)
    rate = lax.rsqrt(row_var + 1e-05)
    return centred * rate, rate


def turned(values):
    lane = lax.broadcasted_iota(jnp.int32, values.shape, 1)
    return jnp.where(
        (lane & 63) < 32, pltpu.roll(values, 96, 1), pltpu.roll(values, 32, 1)
    )


def rotate(values, cosine, sine):
    return values * cosine + turned(values) * sine


def unrotate(values, cosine, sine):
    return values * cosine - turned(values) * sine


def rotary_tables(length, halo):
    half = HD // 2
    inv_freq = (10000.0 ** (-(np.arange(half, dtype=np.float32) * 2.0 / HD))).astype(np.float32)
    place = np.arange(-halo, length, dtype=np.float32)
    angles = place[:, None] * inv_freq[None, :]
    cosine = np.cos(angles.astype(np.float64)).astype(np.float32)
    sine = np.sin(angles.astype(np.float64)).astype(np.float32)
    return (
        np.concatenate([cosine] * 4, axis=1),
        np.concatenate([-sine, sine, -sine, sine], axis=1),
    )


def qkv_kernel(far_ref, near_ref, own_ref, gain_ref, bias_ref, w_ref, cos_ref, sin_ref,
               q_ref, kv_ref, hi_ref, lo_ref):
    step = pl.program_id(0)
    rows = own_ref.shape[0]
    third = pl.num_programs(0) // 3
    halo = hi_ref.shape[0] - rows

    @pl.when(step == 0)
    def _():
        for at, ref in enumerate((far_ref, near_ref, own_ref)):
            xhat, _ = norm_stats(ref[...])
            high, low = split(xhat * gain_ref[...] + bias_ref[...])
            hi_ref[at * rows:(at + 1) * rows] = high
            lo_ref[at * rows:(at + 1) * rows] = low

    weights = split(w_ref[...])

    @pl.when(step < third)
    def _():
        got = three(dot_nn, (hi_ref[halo:], lo_ref[halo:]), weights)
        for at in range(0, got.shape[1], 128):
            q_ref[:, at:at + 128] = rotate(got[:, at:at + 128], cos_ref[halo:], sin_ref[halo:])

    @pl.when((step >= third) & (step < 2 * third))
    def _():
        got = three(dot_nn, (hi_ref[...], lo_ref[...]), weights)
        for at in range(0, got.shape[1], 128):
            kv_ref[:, at:at + 128] = rotate(got[:, at:at + 128], cos_ref[...], sin_ref[...])

    @pl.when(step >= 2 * third)
    def _():
        kv_ref[...] = three(dot_nn, (hi_ref[...], lo_ref[...]), weights)


def project(far, near, own, gain, bias, w_full, cosine, sine):
    rows, model = own.shape
    total = 3 * rows
    wide = 256
    third = model // wide
    whole = lambda shape: pl.BlockSpec(shape, lambda j: (0, 0))
    return pl.pallas_call(
        qkv_kernel,
        grid=(3 * third,),
        in_specs=[
            whole((rows, model)), whole((rows, model)), whole((rows, model)),
            whole((1, model)), whole((1, model)),
            pl.BlockSpec((model, wide), lambda j: (0, j)),
            whole((total, 128)), whole((total, 128)),
        ],
        out_specs=[
            pl.BlockSpec((rows, wide), lambda j: (0, jnp.minimum(j, third - 1))),
            pl.BlockSpec((total, wide), lambda j: (0, jnp.maximum(j - third, 0))),
            whole((total, model)), whole((total, model)),
        ],
        out_shape=[
            jax.ShapeDtypeStruct((rows, model), F32),
            jax.ShapeDtypeStruct((total, 2 * model), F32),
            jax.ShapeDtypeStruct((total, model), BF16),
            jax.ShapeDtypeStruct((total, model), BF16),
        ],
        compiler_params=params(),
    )(far, near, own, gain, bias, w_full, cosine, sine)


def own_pair(values, head):
    lane = lax.broadcasted_iota(jnp.int32, values.shape, 1)
    other = pltpu.roll(values, 64, 1)
    return jnp.where((lane < 64) == (head == 0), values, other)


def outer_form(values, head):
    high, low = split(own_pair(values, head))
    return jnp.concatenate([high, low], axis=1)


def mixed(values, head):
    pair = own_pair(values, head)
    lane = lax.broadcasted_iota(jnp.int32, pair.shape, 1)
    high = pair.astype(BF16).astype(F32)
    return jnp.where(lane < 64, high, pair - high).astype(BF16)


def inner_form(values, head):
    half = mixed(values, head)
    return jnp.concatenate([half, half], axis=1)


def fold(values):
    return values + pltpu.roll(values, 64, 1)


def attend_kernel(q_ref, k_ref, v_ref, segq_ref, segk_ref, out_ref, bias_ref):
    rows = q_ref.shape[0]
    halo = k_ref.shape[0] - rows
    span = halo + BLK

    @pl.when(pl.program_id(0) == 0)
    def _():
        for at in range(0, rows, BLK):
            row = lax.broadcasted_iota(jnp.int32, (BLK, span), 0)
            col = lax.broadcasted_iota(jnp.int32, (BLK, span), 1)
            same = segq_ref[at:at + BLK, :1] == segk_ref[:1, at:at + span]
            bias_ref[at:at + BLK] = jnp.where(same & (col - halo <= row), 0.0, NEG)

    lane = lax.broadcasted_iota(jnp.int32, (BLK, 128), 1)
    scaled = q_ref[...] * (SCALE * LOG2E)
    results = []
    for head in range(2):
        left = inner_form(scaled, head)
        right = outer_form(k_ref[...], head)
        vals = mixed(v_ref[...], head)
        outs = []
        for at in range(0, rows, BLK):
            scores = dot_nt(left[at:at + BLK], right[at:at + span]) + bias_ref[at:at + BLK]
            top = jnp.max(scores, axis=1, keepdims=True)
            expo = jnp.exp2(scores - top)
            total = jnp.sum(expo, axis=1, keepdims=True)
            high, low = split(expo)
            got = dot_nn(high, vals[at:at + span]) + dot_nn(low, vals[at:at + span])
            outs.append(fold(got) / total)
        results.append(outs)
    for at in range(0, rows, BLK):
        out_ref[at:at + BLK] = jnp.where(
            lane < 64, results[0][at // BLK], results[1][at // BLK]
        )


def attend(q_rot, kv, seg_q, seg_k):
    rows, model = q_rot.shape
    total = kv.shape[0]
    pairs = model // 128
    return pl.pallas_call(
        attend_kernel,
        grid=(pairs,),
        in_specs=[
            pl.BlockSpec((rows, 128), lambda p: (0, p)),
            pl.BlockSpec((total, 128), lambda p: (0, p)),
            pl.BlockSpec((total, 128), lambda p: (0, pairs + p)),
            pl.BlockSpec((rows, 128), lambda p: (0, 0)),
            pl.BlockSpec((8, total), lambda p: (0, 0)),
        ],
        out_specs=pl.BlockSpec((rows, 128), lambda p: (0, p)),
        out_shape=jax.ShapeDtypeStruct((rows, model), F32),
        scratch_shapes=[pltpu.VMEM((rows, total - rows + BLK), F32)],
        compiler_params=params(),
    )(q_rot, kv, kv, seg_q, seg_k)


def attend_back_kernel(q_ref, k_ref, v_ref, g_ref, segq_ref, segk_ref, cos_ref, sin_ref,
                       dq_ref, dk_ref, dv_ref, bias_ref):
    rows = q_ref.shape[0]
    halo = k_ref.shape[0] - rows
    span = halo + BLK

    @pl.when(pl.program_id(0) == 0)
    def _():
        for at in range(0, rows, BLK):
            key = lax.broadcasted_iota(jnp.int32, (span, BLK), 0)
            query = lax.broadcasted_iota(jnp.int32, (span, BLK), 1)
            same = segk_ref[at:at + span, :1] == segq_ref[:1, at:at + BLK]
            bias_ref[:, at:at + BLK] = jnp.where(same & (key - halo <= query), 0.0, NEG)

    scaled = q_ref[...] * (SCALE * LOG2E)
    dq, dk, dv = [], [], []
    for head in range(2):
        q_in = inner_form(scaled, head)
        g_in = inner_form(g_ref[...], head)
        k_out = outer_form(k_ref[...], head)
        v_out = outer_form(v_ref[...], head)
        q_mix = mixed(q_ref[...], head)
        g_mix = mixed(g_ref[...], head)
        k_mix = mixed(k_ref[...], head)
        dq_head = []
        dk_head = jnp.zeros((halo + rows, 128), F32)
        dv_head = jnp.zeros((halo + rows, 128), F32)
        dk_parts, dv_parts = [], []
        for at in range(0, rows, BLK):
            scores = dot_nt(k_out[at:at + span], q_in[at:at + BLK]) + bias_ref[:, at:at + BLK]
            top = jnp.max(scores, axis=0, keepdims=True)
            expo = jnp.exp2(scores - top)
            inverse = 1.0 / jnp.sum(expo, axis=0, keepdims=True)
            grad_probs = dot_nt(v_out[at:at + span], g_in[at:at + BLK])
            probs = expo * inverse
            delta = jnp.sum(probs * grad_probs, axis=0, keepdims=True)
            grad_scores = probs * (grad_probs - delta)
            probs_cat = jnp.concatenate(split(probs), axis=1)
            scores_cat = jnp.concatenate(split(grad_scores), axis=1)
            g_two = jnp.concatenate([g_mix[at:at + BLK]] * 2, axis=0)
            q_two = jnp.concatenate([q_mix[at:at + BLK]] * 2, axis=0)
            dv_parts.append(dot_nn(probs_cat, g_two))
            dk_parts.append(dot_nn(scores_cat, q_two))
            got = dot_tn(scores_cat, k_mix[at:at + span])
            dq_head.append(fold(got[:BLK] + got[BLK:]))
        for parts, full in ((dk_parts, dk), (dv_parts, dv)):
            pieces = []
            for kb in range((halo + rows) // BLK):
                terms = [
                    parts[qb][(kb - qb) * BLK:(kb - qb + 1) * BLK]
                    for qb in range(rows // BLK)
                    if 0 <= kb - qb < span // BLK
                ]
                pieces.append(fold(functools.reduce(lambda a, b: a + b, terms)))
            full.append(pieces)
        dq.append(dq_head)
    lane = lax.broadcasted_iota(jnp.int32, (BLK, 128), 1)
    for qb in range(rows // BLK):
        rng = slice(qb * BLK, (qb + 1) * BLK)
        far = slice(halo + qb * BLK, halo + (qb + 1) * BLK)
        both = jnp.where(lane < 64, dq[0][qb], dq[1][qb]) * SCALE
        dq_ref[rng] = unrotate(both, cos_ref[far], sin_ref[far])
    for kb in range((halo + rows) // BLK):
        rng = slice(kb * BLK, (kb + 1) * BLK)
        both = jnp.where(lane < 64, dk[0][kb], dk[1][kb]) * SCALE
        dk_ref[rng] = unrotate(both, cos_ref[rng], sin_ref[rng])
        dv_ref[rng] = jnp.where(lane < 64, dv[0][kb], dv[1][kb])


def attend_back(q_rot, kv, grad, seg_q, seg_k, cosine, sine):
    rows, model = q_rot.shape
    total = kv.shape[0]
    pairs = model // 128
    fixed = lambda shape: pl.BlockSpec(shape, lambda p: (0, 0))
    dq, dk, dv = pl.pallas_call(
        attend_back_kernel,
        grid=(pairs,),
        in_specs=[
            pl.BlockSpec((rows, 128), lambda p: (0, p)),
            pl.BlockSpec((total, 128), lambda p: (0, p)),
            pl.BlockSpec((total, 128), lambda p: (0, pairs + p)),
            pl.BlockSpec((rows, 128), lambda p: (0, p)),
            fixed((8, rows)), fixed((total, 128)),
            fixed((total, 128)), fixed((total, 128)),
        ],
        out_specs=[
            pl.BlockSpec((rows, 128), lambda p: (0, p)),
            pl.BlockSpec((total, 128), lambda p: (0, p)),
            pl.BlockSpec((total, 128), lambda p: (0, p)),
        ],
        out_shape=[
            jax.ShapeDtypeStruct((rows, model), F32),
            jax.ShapeDtypeStruct((total, model), F32),
            jax.ShapeDtypeStruct((total, model), F32),
        ],
        scratch_shapes=[pltpu.VMEM((total - rows + BLK, rows), F32)],
        compiler_params=params(),
    )(q_rot, kv, kv, grad, seg_q, seg_k, cosine, sine)
    return dq, dk, dv


def mlp_kernel(resid_ref, cot_ref, gain_ref, bias_ref, scale_ref, up_ref, down_ref,
               out_ref, gnorm_ref, gup_ref, gdown_ref,
               x_hi, x_lo, xt_hi, xt_lo, g_hi, g_lo):
    step = pl.program_id(0)

    @pl.when(step == 0)
    def _():
        xhat, _ = norm_stats(resid_ref[...])
        normed = xhat * gain_ref[...] + bias_ref[...]
        x_hi[...], x_lo[...] = split(normed)
        xt_hi[...], xt_lo[...] = split(normed.T)
        g_hi[...], g_lo[...] = split(cot_ref[...] * scale_ref[0, 0])
        out_ref[...] = jnp.zeros_like(out_ref)
        gnorm_ref[...] = jnp.zeros_like(gnorm_ref)

    up = split(up_ref[...])
    down = split(down_ref[...])
    normed = (x_hi[...], x_lo[...])
    normed_t = (xt_hi[...], xt_lo[...])
    grad_block = (g_hi[...], g_lo[...])
    pre = three(dot_nn, normed, up)
    grad_act = three(dot_nt, grad_block, down)
    inner = 0.7978845608028654 * (pre + 0.044715 * pre * pre * pre)
    bent = jnp.tanh(inner)
    act = 0.5 * pre * (1.0 + bent)
    slope = 0.5 * (1.0 + bent) + 0.5 * pre * (1.0 - bent * bent) * (
        0.7978845608028654 * (1.0 + 3.0 * 0.044715 * pre * pre)
    )
    act2 = split(act)
    grad_pre = split(grad_act * slope)
    out_ref[...] += three(dot_nn, act2, down)
    gnorm_ref[...] += three(dot_nt, grad_pre, up)
    gdown_ref[...] = three(dot_tn, act2, grad_block)
    gup_ref[...] = three(dot_nn, normed_t, grad_pre)


def mlp(resid, cotangent, gain, bias, scale, up_full, down_full):
    rows, model = resid.shape
    hidden = up_full.shape[1]
    wide = 256
    fixed = lambda shape: pl.BlockSpec(shape, lambda j: (0, 0))
    return pl.pallas_call(
        mlp_kernel,
        grid=(hidden // wide,),
        in_specs=[
            fixed((rows, model)), fixed((rows, model)),
            fixed((1, model)), fixed((1, model)),
            pl.BlockSpec(memory_space=pltpu.SMEM),
            pl.BlockSpec((model, wide), lambda j: (0, j)),
            pl.BlockSpec((wide, model), lambda j: (j, 0)),
        ],
        out_specs=[
            fixed((rows, model)), fixed((rows, model)),
            pl.BlockSpec((model, wide), lambda j: (0, j)),
            pl.BlockSpec((wide, model), lambda j: (j, 0)),
        ],
        out_shape=[
            jax.ShapeDtypeStruct((rows, model), F32),
            jax.ShapeDtypeStruct((rows, model), F32),
            jax.ShapeDtypeStruct((model, hidden), F32),
            jax.ShapeDtypeStruct((hidden, model), F32),
        ],
        scratch_shapes=[
            pltpu.VMEM((rows, model), BF16), pltpu.VMEM((rows, model), BF16),
            pltpu.VMEM((model, rows), BF16), pltpu.VMEM((model, rows), BF16),
            pltpu.VMEM((rows, model), BF16), pltpu.VMEM((rows, model), BF16),
        ],
        compiler_params=params(),
    )(resid, cotangent, gain, bias, scale, up_full, down_full)


def norm_back(grad, gain, xhat, rate):
    scaled = grad * gain
    return rate * (
        scaled
        - jnp.mean(scaled, axis=-1, keepdims=True)
        - xhat * jnp.mean(scaled * xhat, axis=-1, keepdims=True)
    )


def matmul(left, right):
    return jnp.dot(left, right, precision=HIGH)


def inner_rows(left, right):
    return lax.dot_general(left, right, (((0,), (0,)), ((), ())), precision=HIGH)


def outer_cols(left, right):
    return lax.dot_general(left, right, (((1,), (1,)), ((), ())), precision=HIGH)


def body(
    block_input,
    embedding,
    earlier_outs,
    dwa_weights,
    ln1_gain,
    ln1_bias,
    w_qkv,
    w_out,
    ln2_gain,
    ln2_bias,
    w_up,
    w_down,
    segments,
    cotangent,
):
    groups = lax.axis_size("seq")
    rows, model = block_input.shape
    length = rows * groups
    halo = 2 * rows
    place = lax.axis_index("seq")
    ahead = [(i, i + 1) for i in range(groups - 1)]
    behind = [(i + 1, i) for i in range(groups - 1)]
    gain1, bias1 = ln1_gain[None], ln1_bias[None]
    gain2, bias2 = ln2_gain[None], ln2_bias[None]

    gather = lambda v: lax.all_gather(v, "dp", axis=0, tiled=True)
    qkv_full = gather(w_qkv)
    seg_own = segments + 1
    near = lax.ppermute(block_input, "seq", ahead)
    seg_near = lax.ppermute(seg_own, "seq", ahead)
    far = lax.ppermute(near, "seq", ahead)
    seg_far = lax.ppermute(seg_near, "seq", ahead)
    seg_all = jnp.concatenate([seg_far, seg_near, seg_own], axis=1)
    seg_k_row = jnp.broadcast_to(seg_all, (8, halo + rows))
    seg_k_col = jnp.broadcast_to(seg_all.reshape(-1, 1), (halo + rows, 128))
    seg_q_row = seg_k_row[:, halo:]
    seg_q_col = seg_k_col[halo:]

    cos_all, sin_all = rotary_tables(length, halo)
    cosine = lax.dynamic_slice_in_dim(jnp.asarray(cos_all), place * rows, halo + rows, 0)
    sine = lax.dynamic_slice_in_dim(jnp.asarray(sin_all), place * rows, halo + rows, 0)

    q_rot, kv, normed_hi, normed_lo = project(
        far, near, block_input, gain1, bias1, qkv_full, cosine, sine
    )
    attended = attend(q_rot, kv, seg_q_col, seg_k_row)

    out_full = gather(w_out)
    up_full = gather(w_up)
    down_full = gather(w_down)
    resid = block_input + matmul(attended, out_full)
    mlp_out, grad_normed_two, grad_up_part, grad_down_part = mlp(
        resid, cotangent, gain2, bias2, dwa_weights[4].reshape(1, 1), up_full, down_full
    )
    scatter = lambda v: lax.psum_scatter(v, "dp", scatter_dimension=0, tiled=True)
    up_shard, down_shard = scatter(grad_up_part), scatter(grad_down_part)

    block_out = resid + mlp_out
    output = (
        dwa_weights[0] * embedding
        + dwa_weights[1] * earlier_outs[0]
        + dwa_weights[2] * earlier_outs[1]
        + dwa_weights[3] * earlier_outs[2]
        + dwa_weights[4] * block_out
    )
    dwa_local = jnp.stack(
        [
            jnp.sum(cotangent * embedding),
            jnp.sum(cotangent * earlier_outs[0]),
            jnp.sum(cotangent * earlier_outs[1]),
            jnp.sum(cotangent * earlier_outs[2]),
            jnp.sum(cotangent * block_out),
        ]
    )
    xhat2, rate2 = norm_stats(resid)
    grad_resid = dwa_weights[4] * cotangent + norm_back(grad_normed_two, gain2, xhat2, rate2)
    grad_gain_two = jnp.sum(grad_normed_two * xhat2, axis=0)
    grad_bias_two = jnp.sum(grad_normed_two, axis=0)
    grad_attended = outer_cols(grad_resid, out_full)
    grad_wout_part = inner_rows(attended, grad_resid)

    dq, dk, dv = attend_back(
        q_rot, kv, grad_attended, seg_q_row, seg_k_col, cosine, sine
    )
    normed_one = normed_hi.astype(F32) + normed_lo.astype(F32)
    dkv = jnp.concatenate([dk, dv], axis=1)
    grad_qkv_part = jnp.concatenate(
        [inner_rows(normed_one[halo:], dq), inner_rows(normed_one, dkv)], axis=1
    )
    wout_shard, qkv_shard = scatter(grad_wout_part), scatter(grad_qkv_part)

    wq, wkv = qkv_full[:, :model], qkv_full[:, model:]
    partial = outer_cols(dkv, wkv)
    own_part = partial[halo:] + outer_cols(dq, wq)
    back_near = partial[rows:halo] + lax.ppermute(partial[:rows], "seq", behind)
    grad_normed_one = own_part + lax.ppermute(back_near, "seq", behind)
    xhat1, rate1 = norm_stats(block_input)
    grad_input = grad_resid + norm_back(grad_normed_one, gain1, xhat1, rate1)
    grad_gain_one = jnp.sum(grad_normed_one * xhat1, axis=0)
    grad_bias_one = jnp.sum(grad_normed_one, axis=0)

    grad_up, grad_down = lax.psum((up_shard, down_shard), "seq")
    grad_qkv, grad_wout = lax.psum((qkv_shard, wout_shard), "seq")
    gain_one, bias_one, gain_two, bias_two, grad_dwa = lax.psum(
        (grad_gain_one, grad_bias_one, grad_gain_two, grad_bias_two, dwa_local), ("dp", "seq")
    )
    return (
        output,
        grad_input,
        grad_dwa,
        gain_one,
        bias_one,
        grad_qkv,
        grad_wout,
        gain_two,
        bias_two,
        grad_up,
        grad_down,
    )


def solution(mesh):
    in_specs = (
        P(("dp", "seq"), None),
        P(("dp", "seq"), None),
        P(None, ("dp", "seq"), None),
        P(),
        P(),
        P(),
        P("dp", None),
        P("dp", None),
        P(),
        P(),
        P("dp", None),
        P("dp", None),
        P("dp", "seq"),
        P(("dp", "seq"), None),
    )
    out_specs = (
        P(("dp", "seq"), None),
        P(("dp", "seq"), None),
        P(),
        P(),
        P(),
        P("dp", None),
        P("dp", None),
        P(),
        P(),
        P("dp", None),
        P("dp", None),
    )
    return jax.shard_map(body, mesh=mesh, in_specs=in_specs, out_specs=out_specs, check_vma=False)
```

time: 1130 us -> 759 us (0.67); the launches traced: 1110 us -> 756 us
  matrix products: 405 us -> 42.8 us
  Pallas kernels: 0 us -> 147 us
  blocking collectives: 190 us -> 43.9 us
  waiting for transfers between devices: 297 us -> 437 us
  local copies, waits for them, and re-layouts: 133 us -> 26 us
    dot_general x33 -> x7, matrix products: 405 us -> 42.8 us  [the longest x3 20.7 us: outer_cols(): lax.dot_general(left, right, (((1,), (1,)), ((), ())), precision=HIGH)]
    pallas_call x0 -> x4, Pallas kernels: none -> 147 us  [the longest x1 59.1 us: mlp(): pl.pallas_call(mlp_kernel, grid=(hidden // wide,), in_specs=[fixed((rows,...]
    all_to_all x1 -> x0, blocking collectives: 145 us -> none  [body(): lax.all_to_all(grad_heads_qkv, 'seq', split_axis=0, concat_axis=2, tiled=...]
    reduce_scatter x4, waiting for transfers between devices: 63.7 us -> 208 us  [body(): lax.psum_scatter(v, 'dp', scatter_dimension=0, tiled=True)]
    all_to_all x4 -> x0, waiting for transfers between devices: 120 us -> none  [the longest x1 88.6 us: body(): lax.all_to_all(packed, 'seq', split_axis=2, concat_axis=0, tiled=True)]
    ppermute x0 -> x6, waiting for transfers between devices: none -> 113 us  [the longest x1 70.5 us: body(): grad_normed_one = own_part + lax.ppermute(back_near, 'seq', behind)]
    dynamic_update_slice x12 -> x0, local copies, waits for them, and re-layouts: 56.6 us -> none  [body(): lax.map(attend, jnp.arange(block_count, dtype=jnp.int32))]
    all_gather x4, waiting for transfers between devices: 44.7 us -> 84.5 us  [body(): gather = lambda v: lax.all_gather(v, 'dp', axis=0, tiled=True)]
  transfers between devices with their start and end apart: 13 -> 15, of which waited for: 6 -> 9; matrix products, arithmetic and copies ran while one was open for 44% -> 9% of each run, Pallas kernels for 0% -> 12%
where the time goes in v1:
time: 759 us; the launch traced here: 756 us
  waiting for transfers between devices  437 us (58%)
  Pallas kernels  147 us (19%)
  blocking collectives  43.9 us (6%)
  matrix products  42.8 us (6%)
  local copies, waits for them, and re-layouts  26 us (3%)
  other arithmetic  23.9 us (3%)
  starting transfers between devices  21 us (3%)
  between operations  14.5 us (2%)
    reduce_scatter x4, waiting for transfers between devices, body(): lax.psum_scatter(v, 'dp', scatter_dimension=0, tiled=True)  208 us
    all_gather x4, waiting for transfers between devices, body(): gather = lambda v: lax.all_gather(v, 'dp', axis=0, tiled=True)  84.5 us
    ppermute x1, waiting for transfers between devices, body(): grad_normed_one = own_part + lax.ppermute(back_near, 'seq', behind)  70.5 us
    pallas_call x1, Pallas kernels, mlp(): pl.pallas_call(mlp_kernel, grid=(hidden // wide,), in_specs=[fixed((rows,...  59.1 us
    psum x1, blocking collectives, body(): lax.psum((grad_gain_one, grad_bias_one, grad_gain_two, grad_bias_two, dwa...  43.9 us
    pallas_call x1, Pallas kernels, attend_back(): pl.pallas_call(attend_back_kernel, grid=(pairs,), in_specs=[pl.BlockSpec(...  43.5 us
    psum x1, waiting for transfers between devices, body(): grad_qkv, grad_wout = lax.psum((qkv_shard, wout_shard), 'seq')  27.2 us
    ppermute x1, waiting for transfers between devices, body(): near = lax.ppermute(block_input, 'seq', ahead)  25.1 us
  transfers between devices with their start and end apart: 15, of which 9 were waited for; matrix products, arithmetic and copies ran while one was open for 9% of the time, Pallas kernels for 12%

profile of v1, /device:TPU:0, one launch (start us, length us, event | category | flops | bytes accessed | tf_op | source)
XLA Modules:
  0.0 756.1 jit_solution(16697141901067786563)
XLA Ops:
  10.1 5.0 collective-permute-start
  15.1 25.1 %collective-permute-done.near_ref = f32[384,768]{1,0:T(8,128)S(1)} collective-permute-done((f32[384,768]{1,0:T(8,128)S(1)}, f32[384,768]{1,0:T(8,128)S(1)}, u32[]{:S(2)}, u32[]{:S(2)}) %collective-permute-start) | collective-permute-done | bytes 1179680 | tf_op jit(solution)/shard_map/ppermute | solution.py:459
  40.2 4.4 collective-permute-start.1
  45.3 4.0 collective-permute-start.2
  49.3 2.2 constant_dynamic-slice_fusion
  51.5 17.4 %collective-permute-done.2 = s32[1,384]{1,0:T(1,128)} collective-permute-done((s32[1,384]{1,0:T(1,128)S(1)}, s32[1,384]{1,0:T(1,128)}, u32[]{:S(2)}, u32[]{:S(2)}) %collective-permute-start.2) | collective-permute-done | bytes 1568 | tf_op jit(solution)/shard_map/ppermute | solution.py:460
  69.0 4.5 collective-permute-start.3
  76.4 0.7 add_reduce_fusion
  77.2 1.0 copy-done.19
  78.2 21.6 %shard_map.239 = (f32[384,768]{1,0:T(8,128)}, f32[1152,1536]{1,0:T(8,128)}, bf16[1152,768]{1,0:T(8,128)(2,1)}, bf16[1152,768]{1,0:T(8,128)(2,1)}) custom-call(f32[384,768]{1,0:T(8,128)} %copy-done.19, f32[384,768]{1,0:T(8,128)} %copy-done.18, f32[384,768]{1,0:T(8,128)} %own_ref.1, f32[1,768]{1,0:T(1,128)} %broadcast_in_dim.36.gain_ref, ...), custom_call_target="tpu_custom_call" | custom-call | tf_op jit(solution)/shard_map/pallas_call | solution.py:129
  99.8 0.8 broadcast_in_dim.38.segq_ref
  101.2 23.2 %shard_map.240 = f32[384,768]{1,0:T(8,128)} custom-call(f32[384,768]{1,0:T(8,128)} %get-tuple-element.22.q_ref, f32[1152,1536]{1,0:T(8,128)} %get-tuple-element.23.k_ref.v_ref, f32[1152,1536]{1,0:T(8,128)} %get-tuple-element.23.k_ref.v_ref, s32[384,128]{1,0:T(8,128)} %broadcast_in_dim.38.segq_ref, s32[8,1152]{1,0:T(8,128)} %broadcast_in_dim.40.segk_ref), custom_call_target="tpu_custom_call" | custom-call | tf_op jit(solution)/shard_map/pallas_call | solution.py:220
  124.4 3.9 fusion.22
  129.3 23.9 %all-gather.9.cloned.1.call-done.up_ref = f32[768,3072]{1,0:T(8,128)} async-done(((f32[96,3072]{1,0:T(8,128)}), f32[768,3072]{1,0:T(8,128)}) %all-gather.9.cloned.1.call-update) | async-done | bytes 9437200 | tf_op jit(solution)/shard_map/all_gather | solution.py:456
  153.2 60.6 %all-gather.11.cloned.1.call-done.down_ref = f32[3072,768]{1,0:T(8,128)} async-done(((f32[384,768]{1,0:T(8,128)}), f32[3072,768]{1,0:T(8,128)}) %all-gather.11.cloned.1.call-update) | async-done | bytes 9437200 | tf_op jit(solution)/shard_map/all_gather | solution.py:456
  213.8 59.1 %shard_map.241 = (f32[384,768]{1,0:T(8,128)}, f32[384,768]{1,0:T(8,128)}, f32[768,3072]{1,0:T(8,128)}, f32[3072,768]{1,0:T(8,128)}) custom-call(f32[384,768]{1,0:T(8,128)} %copy-done.2, f32[384,768]{1,0:T(8,128)} %cot_ref.1, f32[1,768]{1,0:T(1,128)} %broadcast_in_dim.41.gain_ref, f32[1,768]{1,0:T(1,128)} %broadcast_in_dim.42.bias_ref, ...), custom_call_target="tpu_custom_call" | custom-call | tf_op jit(solution)/shard_map/pallas_call | solution.py:379
  273.1 3.7 multiply_reduce_fusion
  276.8 5.1 multiply_add_fusion.1
  281.9 3.6 fusion.24
  285.6 2.5 convert_add_fusion
  288.3 2.8 fusion.23.g_ref
  291.6 1.0 broadcast_in_dim.44.segk_ref
  292.7 43.5 %shard_map.242 = (f32[384,768]{1,0:T(8,128)}, f32[1152,768]{1,0:T(8,128)}, f32[1152,768]{1,0:T(8,128)}) custom-call(f32[384,768]{1,0:T(8,128)} %get-tuple-element.22.q_ref, f32[1152,1536]{1,0:T(8,128)} %get-tuple-element.23.k_ref.v_ref, f32[1152,1536]{1,0:T(8,128)} %get-tuple-element.23.k_ref.v_ref, f32[384,768]{1,0:T(8,128)} %fusion.23.g_ref, ...), custom_call_target="tpu_custom_call" | custom-call | tf_op jit(solution)/shard_map/pallas_call | solution.py:311
  336.2 3.7 fusion.10
  340.4 1.5 copy-done.13
  342.4 0.9 copy-done.15
  343.9 10.9 %fusion.20 = f32[768,1536]{1,0:T(8,128)S(1)} fusion(f32[1152,1536]{1,0:T(8,128)S(1)} %constant_dynamic-update-slice_fusion, bf16[1152,768]{1,0:T(8,128)(2,1)S(1)} %copy-done.16, bf16[1152,768]{1,0:T(8,128)(2,1)S(1)} %copy-done.15), kind=kOutput, calls=%fused_computation.54 | convolution fusion | flops 8156381184 | bytes 15335424 | tf_op jit(solution)/shard_map/dot_general | solution.py:423
  354.8 3.4 pad_maximum_fusion
  358.3 0.7 reduce-scatter.9.cloned.1.call-update
  359.8 12.2 %fusion = f32[1152,768]{1,0:T(8,128)S(1)} fusion(f32[1152,1536]{1,0:T(8,128)} %copy-done.17, f32[768,2304]{1,0:T(8,128)} %all-gather.5.cloned.1.call-done.w_ref), kind=kOutput, calls=%fused_computation.1 | convolution fusion | flops 8153726976 | bytes 15335424 | tf_op jit(solution)/shard_map/dot_general | solution.py:427
  372.0 1.8 copy-done.12
  373.7 1.1 slice.74
  374.8 1.3 collective-permute-start.4
  376.1 47.7 %reduce-scatter.5.cloned.1.call-done = f32[96,2304]{1,0:T(8,128)} async-done(((f32[768,2304]{1,0:T(8,128)}), f32[96,2304]{1,0:T(8,128)}) %reduce-scatter.5.cloned.1.call-update) | async-done | bytes 884752 | tf_op jit(solution)/shard_map/reduce_scatter | solution.py:485
  423.9 80.0 %reduce-scatter.9.cloned.1.call-done = f32[96,3072]{1,0:T(8,128)} async-done(((f32[768,3072]{1,0:T(8,128)}), f32[96,3072]{1,0:T(8,128)}) %reduce-scatter.9.cloned.1.call-update) | async-done | bytes 1179664 | tf_op jit(solution)/shard_map/reduce_scatter | solution.py:485
  503.9 80.0 %reduce-scatter.11.cloned.1.call-done = f32[384,768]{1,0:T(8,128)} async-done(((f32[3072,768]{1,0:T(8,128)}), f32[384,768]{1,0:T(8,128)}) %reduce-scatter.11.cloned.1.call-update) | async-done | bytes 1179664 | tf_op jit(solution)/shard_map/reduce_scatter | solution.py:485
  583.9 2.4 slice_add_fusion
  586.3 1.4 collective-permute-start.5
  588.2 3.9 stack.23
  592.1 70.5 %collective-permute-done.5 = f32[384,768]{1,0:T(8,128)} collective-permute-done((f32[384,768]{1,0:T(8,128)}, f32[384,768]{1,0:T(8,128)}, u32[]{:S(2)}, u32[]{:S(2)}) %collective-permute-start.5) | collective-permute-done | bytes 1179680 | tf_op jit(solution)/shard_map/ppermute | solution.py:526
  662.6 5.8 multiply_reduce_fusion.1
  668.5 43.9 %all-reduce = (f32[5]{0:T(128)}, f32[768]{0:T(1024)}, f32[768]{0:T(1024)}, f32[768]{0:T(1024)}, f32[768]{0:T(1024)}) all-reduce(f32[5]{0:T(128)} %stack.23, f32[768]{0:T(1024)} %get-tuple-element.38, f32[768]{0:T(1024)} %get-tuple-element.48, f32[768]{0:T(1024)S(1)} %copy-done.31, ...), channel_id=1, replica_groups=mesh['dp'=8,'seq'=4] {'dp','seq'}, use_global_device_ids=true, to_apply=%region_13.0 | all-reduce | flops 3077 | bytes 24616 | tf_op jit(solution)/shard_map/psum | solution.py:534
  713.7 2.7 multiply_add_fusion
  716.4 27.2 %all-reduce.4.cloned.1.call-done = (f32[96,2304]{1,0:T(8,128)}, f32[96,768]{1,0:T(8,128)}, f32[96,3072]{1,0:T(8,128)}, f32[384,768]{1,0:T(8,128)}) async-done(((f32[96,2304]{1,0:T(8,128)}, f32[96,768]{1,0:T(8,128)}, f32[96,3072]{1,0:T(8,128)}, f32[384,768]{1,0:T(8,128)}), (f32[96,2304]{1,0:T(8,128)}, f32[96,768]{1,0:T(8,128)}, f32[96,3072]{1,0:T(8,128)}, f32[384,768]{1,0:T(8,128)})) %all-reduce.4.cloned.1.call-update) | async-done | bytes 3538960 | tf_op jit(solution)/shard_map/psum | solution.py:533
  743.7 2.2 copy.34
  745.9 0.7 copy.35
  746.6 1.0 copy.36
  748.3 1.0 copy.37
  (114 shorter events, 13.9 us)
Async XLA Ops:
  7.2 70.0 %all-gather.5.cloned.1.call-start = ((), (), s32[]{:S(2)}) async-start(), calls=%async_computation.4 | async-start | bytes 7962624 | tf_op jit(solution)/shard_map/all_gather | solution.py:456
  7.9 116.5 %all-gather.7.cloned.1.call-start = ((), (), s32[]{:S(2)}) async-start(), calls=%async_computation.5 | async-start | bytes 2654208 | tf_op jit(solution)/shard_map/all_gather | solution.py:456
  8.0 36.7 %copy-start.36 = (s32[1,384]{1,0:T(1,128)S(1)}, s32[1,384]{1,0:T(1,128)}, u32[]{:S(2)}) copy-start(s32[1,384]{1,0:T(1,128)} %param.28) | copy-start | bytes 4612
  8.7 40.6 %copy-start.22 = (f32[2304,128]{1,0:T(8,128)S(1)}, f32[2304,128]{1,0:T(8,128)}, u32[]{:S(2)}) copy-start(f32[2304,128]{1,0:T(8,128)} %constant.31.clone) | copy-start | bytes 3538948
  8.7 144.5 %all-gather.9.cloned.1.call-start = ((), (), s32[]{:S(2)}) async-start(), calls=%async_computation.6 | async-start | bytes 10616832 | tf_op jit(solution)/shard_map/all_gather | solution.py:456
  9.4 204.4 %all-gather.11.cloned.1.call-start = ((), (), s32[]{:S(2)}) async-start(), calls=%async_computation.7 | async-start | bytes 10616832 | tf_op jit(solution)/shard_map/all_gather | solution.py:456
  10.0 366.1 %reduce-scatter.7.cloned.1.call-start = ((), (), s32[]{:S(2)}) async-start(), calls=%async_computation.9 | async-start | bytes 2654208 | tf_op jit(solution)/shard_map/reduce_scatter | solution.py:485
  10.1 30.1 %collective-permute-start = (f32[384,768]{1,0:T(8,128)S(1)}, f32[384,768]{1,0:T(8,128)S(1)}, u32[]{:S(2)}, u32[]{:S(2)}) collective-permute-start(f32[384,768]{1,0:T(8,128)S(1)} %copy-done), channel_id=1, source_target_pairs={{0,1},{1,2},{2,3},{4,5},{5,6},{6,7},{8,9},{9,10},{10,11},{12,13},{... | collective-permute-start | bytes 3538952 | tf_op jit(solution)/shard_map/ppermute | solution.py:459
  40.2 11.3 %copy-start.18 = (f32[384,768]{1,0:T(8,128)}, f32[384,768]{1,0:T(8,128)S(1)}, u32[]{:S(2)}) copy-start(f32[384,768]{1,0:T(8,128)S(1)} %collective-permute-done.near_ref) | copy-start | bytes 3538948
  40.2 37.0 %collective-permute-start.1 = (f32[384,768]{1,0:T(8,128)S(1)}, f32[384,768]{1,0:T(8,128)S(1)}, u32[]{:S(2)}, u32[]{:S(2)}) collective-permute-start(f32[384,768]{1,0:T(8,128)S(1)} %collective-permute-done.near_ref), channel_id=1, source_target_pairs={{0,1},{1,2},{2,3},{4,5},{5,6},{6,7},{8,9},{9,10},{10,11},{12,13},{... | collective-permute-start | bytes 3538952 | tf_op jit(solution)/shard_map/ppermute | solution.py:461
  45.3 6.2 copy-start.33
  45.3 23.7 %collective-permute-start.2 = (s32[1,384]{1,0:T(1,128)S(1)}, s32[1,384]{1,0:T(1,128)}, u32[]{:S(2)}, u32[]{:S(2)}) collective-permute-start(s32[1,384]{1,0:T(1,128)S(1)} %get-tuple-element.60), channel_id=1, source_target_pairs={{0,1},{1,2},{2,3},{4,5},{5,6},{6,7},{8,9},{9,10},{10,11},{12,13},{... | collective-permute-start | bytes 4616 | tf_op jit(solution)/shard_map/ppermute | solution.py:460
  49.3 24.2 %copy-start.32 = (f32[5]{0:T(128)S(1)}, f32[5]{0:T(128)}, u32[]{:S(2)}) copy-start(f32[5]{0:T(128)} %param.19) | copy-start | bytes 64
  49.3 24.8 %copy-start.25 = (f32[768]{0:T(1024)S(1)}, f32[768]{0:T(1024)}, u32[]{:S(2)}) copy-start(f32[768]{0:T(1024)} %param.20) | copy-start | bytes 9220
  49.3 25.4 %copy-start.34 = (f32[768]{0:T(1024)S(1)}, f32[768]{0:T(1024)}, u32[]{:S(2)}) copy-start(f32[768]{0:T(1024)} %param.21) | copy-start | bytes 9220
  49.3 26.0 %copy-start.24 = (f32[768]{0:T(1024)S(1)}, f32[768]{0:T(1024)}, u32[]{:S(2)}) copy-start(f32[768]{0:T(1024)} %param.24) | copy-start | bytes 9220
  49.3 26.6 %copy-start.35 = (f32[768]{0:T(1024)S(1)}, f32[768]{0:T(1024)}, u32[]{:S(2)}) copy-start(f32[768]{0:T(1024)} %param.25) | copy-start | bytes 9220
  69.0 7.5 collective-permute-start.3
  78.2 21.6 %copy-start.28 = (s32[384]{0:T(512)S(1)}, s32[384]{0:T(512)}, u32[]{:S(2)}) copy-start(s32[384]{0:T(512)} %get-tuple-element.61) | copy-start | bytes 4612
  101.2 23.2 %copy-start.1 = (f32[384,768]{1,0:T(8,128)S(1)}, f32[384,768]{1,0:T(8,128)}, u32[]{:S(2)}) copy-start(f32[384,768]{1,0:T(8,128)} %own_ref.1) | copy-start | bytes 3538948
  128.3 85.5 %copy-start.2 = (f32[384,768]{1,0:T(8,128)}, f32[384,768]{1,0:T(8,128)S(1)}, u32[]{:S(2)}) copy-start(f32[384,768]{1,0:T(8,128)S(1)} %get-tuple-element.68.resid_ref) | copy-start | bytes 3538948
  128.4 85.4 %copy-start.26 = (f32[384]{0:T(512)}, f32[384]{0:T(512)S(1)}, u32[]{:S(2)}) copy-start(f32[384]{0:T(512)S(1)} %broadcast_multiply_fusion.5) | copy-start | bytes 4612
  213.8 59.2 %copy-start.4 = (f32[3,384,768]{2,1,0:T(8,128)S(1)}, f32[3,384,768]{2,1,0:T(8,128)}, u32[]{:S(2)}) copy-start(f32[3,384,768]{2,1,0:T(8,128)} %param.18) | copy-start | bytes 10616836
  213.8 59.2 %copy-start.6 = (f32[384,768]{1,0:T(8,128)S(1)}, f32[384,768]{1,0:T(8,128)}, u32[]{:S(2)}) copy-start(f32[384,768]{1,0:T(8,128)} %cot_ref.1) | copy-start | bytes 3538948
  213.8 59.2 %copy-start.8 = (f32[384,768]{1,0:T(8,128)S(1)}, f32[384,768]{1,0:T(8,128)}, u32[]{:S(2)}) copy-start(f32[384,768]{1,0:T(8,128)} %param.17) | copy-start | bytes 3538948
  213.8 59.2 %copy-start.27 = (f32[384]{0:T(512)S(1)}, f32[384]{0:T(512)}, u32[]{:S(2)}) copy-start(f32[384]{0:T(512)} %copy-done.26) | copy-start | bytes 4612
  213.8 59.2 %copy-start.30 = (f32[384]{0:T(512)S(1)}, f32[384]{0:T(512)}, u32[]{:S(2)}) copy-start(f32[384]{0:T(512)} %add_rsqrt_fusion.1) | copy-start | bytes 4612
  273.0 3.8 copy-start.3
  273.0 3.8 copy-start.10
  273.1 3.8 copy-start.11
  276.8 5.1 copy-start.5
  285.5 138.4 %reduce-scatter.5.cloned.1.call-start = ((), (), s32[]{:S(2)}) async-start(), calls=%async_computation.8 | async-start | bytes 7962624 | tf_op jit(solution)/shard_map/reduce_scatter | solution.py:485
  285.5 2.7 copy-start.7
  288.3 2.8 copy-start.29
  336.2 3.7 copy-start.14
  339.9 2.0 copy-start.13
  341.9 2.0 copy-start.16
  343.9 10.9 %copy-start.17 = (f32[1152,1536]{1,0:T(8,128)}, f32[1152,1536]{1,0:T(8,128)S(1)}, u32[]{:S(2)}) copy-start(f32[1152,1536]{1,0:T(8,128)S(1)} %constant_dynamic-update-slice_fusion) | copy-start | bytes 21233668
  358.2 145.7 %reduce-scatter.9.cloned.1.call-start = ((), (), s32[]{:S(2)}) async-start(), calls=%async_computation.10 | async-start | bytes 10616832 | tf_op jit(solution)/shard_map/reduce_scatter | solution.py:485
  359.0 224.9 %reduce-scatter.11.cloned.1.call-start = ((), (), s32[]{:S(2)}) async-start(), calls=%async_computation.11 | async-start | bytes 10616832 | tf_op jit(solution)/shard_map/reduce_scatter | solution.py:485
  359.7 383.9 %all-reduce.4.cloned.1.call-start = ((), (), s32[]{:S(2)}) async-start(), calls=%async_computation.12 | async-start | bytes 7077888 | tf_op jit(solution)/shard_map/psum | solution.py:533
  371.9 1.8 copy-start.12
  374.8 209.1 %collective-permute-start.4 = (f32[384,768]{1,0:T(8,128)}, f32[384,768]{1,0:T(8,128)S(1)}, u32[]{:S(2)}, u32[]{:S(2)}) collective-permute-start(f32[384,768]{1,0:T(8,128)} %slice.74), channel_id=1, source_target_pairs={{1,0},{2,1},{3,2},{5,4},{6,5},{7,6},{9,8},{10,9},{11,10},{13,12},{... | collective-permute-start | bytes 3538952 | tf_op jit(solution)/shard_map/ppermute | solution.py:525
  586.3 76.3 %copy-start.9 = (f32[384,768]{1,0:T(8,128)S(1)}, f32[384,768]{1,0:T(8,128)}, u32[]{:S(2)}) copy-start(f32[384,768]{1,0:T(8,128)} %get-tuple-element.28) | copy-start | bytes 3538948
  586.3 76.3 %collective-permute-start.5 = (f32[384,768]{1,0:T(8,128)}, f32[384,768]{1,0:T(8,128)}, u32[]{:S(2)}, u32[]{:S(2)}) collective-permute-start(f32[384,768]{1,0:T(8,128)} %slice_add_fusion), channel_id=1, source_target_pairs={{1,0},{2,1},{3,2},{5,4},{6,5},{7,6},{9,8},{10,9},{11,10},{13,12},{... | collective-permute-start | bytes 3538952 | tf_op jit(solution)/shard_map/ppermute | solution.py:526
  592.1 76.3 %copy-start.31 = (f32[768]{0:T(1024)S(1)}, f32[768]{0:T(1024)}, u32[]{:S(2)}) copy-start(f32[768]{0:T(1024)} %get-tuple-element.36) | copy-start | bytes 9220
  743.7 2.3 copy-start.23
  743.7 3.0 copy-start.21
  (4 other events, 5.6 us)
Sparse Core Ops, SparseCore 0:
  9.9 51.5 all-gather.4
  63.4 29.0 all-gather.6
  94.3 58.8 all-gather.8
  154.9 58.8 all-gather.10
  285.6 42.4 reduce-scatter.6
  358.3 65.4 reduce-scatter.4
  427.4 76.4 reduce-scatter.8
  507.4 76.4 reduce-scatter.10
  586.5 157.0 all-reduce.3
